TPU v7x, 128 devices: a whole 4x4x4 slice. The times are simulated.
128 devices in a mesh: dom: 4 (over x), head: 32 (over z, y, core).
Axes of the slice: x: 4, y: 4, z: 4, core: 2. Of those that a mesh axis runs over, the one named last changes fastest.
Arguments:
- tokens: bfloat16 [24, 64, 8192], P(None, 'dom', 'head'), may hold values from -6 to 6
- parents: int32 [64], replicated, may hold values from 0 to 63, as said below
- recurrent_state: float32 [64, 128, 64, 256], P('dom', 'head'), may hold values from -6 to 6
- value_history: float32 [64, 3, 8192], P('dom', None, 'head'), may hold values from -6 to 6
- mixing_history: float32 [64, 3, 2048], P('dom', None, 'head'), may hold values from -6 to 6
- input_gain: float32 [8192], P('head'), may hold values from 0.5 to 1.5
- gate_value_weight: bfloat16 [8192, 2, 8192], P(None, None, 'head'), may hold values from -0.0625 to 0.0625
- mixing_weight: bfloat16 [8192, 2048], P(None, 'head'), may hold values from -0.0625 to 0.0625
- step_weight: bfloat16 [8192, 128], P(None, 'head'), may hold values from -0.0625 to 0.0625
- value_kernel: float32 [4, 8192], P(None, 'head'), may hold values from -3 to 3
- value_offset: float32 [8192], P('head'), may hold values from -0.5 to 0.5
- mixing_kernel: float32 [4, 2048], P(None, 'head'), may hold values from -3 to 3
- mixing_offset: float32 [2048], P('head'), may hold values from -0.5 to 0.5
- step_offset: float32 [128], P('head'), may hold values from -4 to 0
- decay_log: float32 [128], P('head'), may hold values from -2 to 1.5
- skip_gain: float32 [128], P('head'), may hold values from 0.5 to 1.5
- output_gain: float32 [8192], P('head'), may hold values from 0.5 to 1.5
- output_weight: bfloat16 [8192, 8192], P('head'), may hold values from -0.0625 to 0.0625
Outputs:
- mixed: bfloat16 [24, 64, 8192], P(None, 'dom', 'head')
Inputs may be any that keep to these rules, and one draw needn't show every extreme that they name: parents comes from systematic resampling: it never falls with i, and offspring counts are very uneven, so that a particle's parent may sit several blocks of 16 particles away.
All inputs are finite; a program needn't handle non-finite values.
Results may differ from a plain program's by a relative error of at most 0.023.
Values may be sent and summed in bfloat16 or wider, within the bound.
A program may use at most 128 MiB of HBM per device.

v0:
```python
import jax
import jax.numpy as jnp
from jax import lax
from jax.sharding import PartitionSpec as P

HEADS = 128
GROUPS = 4
P_SIZE = 64


def causal_conv(previous, current, kernel, shift_bias):
    window = jnp.concatenate([jnp.moveaxis(previous, 1, 0), current], axis=0)
    length = current.shape[0]
    summed = jnp.zeros_like(current)
    for tap_index in range(kernel.shape[0]):
        summed = summed + kernel[tap_index] * window[tap_index : tap_index + length]
    return jax.nn.silu(summed + shift_bias)


def pick_rows(carried, pieces, wanted):
    counted = pieces[0].shape[0]
    inside = (wanted >= 0) & (wanted < counted)
    safe_rows = jnp.clip(wanted, 0, counted - 1)
    result = []
    for held_rows, source in zip(carried, pieces):
        taken_rows = jnp.take(source, safe_rows, axis=0)
        mask_shape = (wanted.shape[0],) + (1,) * (source.ndim - 1)
        result.append(jnp.where(inside.reshape(mask_shape), taken_rows, held_rows))
    return tuple(result)


def body(
    tokens,
    parents,
    recurrent_state,
    value_history,
    mixing_history,
    input_gain,
    gate_value_weight,
    mixing_weight,
    step_weight,
    value_kernel,
    value_offset,
    mixing_kernel,
    mixing_offset,
    step_offset,
    decay_log,
    skip_gain,
    output_gain,
    output_weight,
):
    steps_count, local_particles, local_width = tokens.shape
    local_heads, head_width, state_width = (
        recurrent_state.shape[1],
        recurrent_state.shape[2],
        recurrent_state.shape[3],
    )
    channels = local_heads * head_width
    row_count = steps_count * local_particles
    dom_index = lax.axis_index("dom")
    head_count = lax.axis_size("head")
    head_index = lax.axis_index("head")
    gathered, full_gain = (
        lax.all_gather(tokens, "head", axis=2, tiled=True),
        lax.all_gather(input_gain.astype(jnp.bfloat16), "head", axis=0, tiled=True).astype(
            input_gain.dtype
        ),
    )
    flat_tokens = gathered.astype(jnp.float32).reshape(row_count, -1)
    normed = (
        flat_tokens
        * lax.rsqrt(jnp.mean(flat_tokens * flat_tokens, axis=-1, keepdims=True) + 1e-05)
        * full_gain
    ).astype(jnp.bfloat16)
    gate_value = jnp.dot(
        normed,
        gate_value_weight.reshape(gate_value_weight.shape[0], 2 * channels),
        preferred_element_type=jnp.float32,
    ).reshape(steps_count, local_particles, 2, channels)
    mixing_raw = jnp.dot(normed, mixing_weight, preferred_element_type=jnp.float32).reshape(
        steps_count, local_particles, -1
    )
    step_raw = jnp.dot(normed, step_weight, preferred_element_type=jnp.float32).reshape(
        steps_count, local_particles, local_heads
    )
    first_child = dom_index * local_particles
    own_parents = lax.dynamic_slice_in_dim(parents, first_child, local_particles)
    initial = (
        jnp.zeros_like(recurrent_state),
        jnp.zeros_like(value_history),
        jnp.zeros_like(mixing_history),
    )
    start_state, value_prev, mixing_prev = pick_rows(
        initial,
        (
            lax.all_gather(recurrent_state.astype(jnp.bfloat16), "dom", axis=0, tiled=True).astype(
                jnp.float32
            ),
            lax.all_gather(value_history.astype(jnp.bfloat16), "dom", axis=0, tiled=True).astype(
                jnp.float32
            ),
            lax.all_gather(mixing_history.astype(jnp.bfloat16), "dom", axis=0, tiled=True).astype(
                jnp.float32
            ),
        ),
        own_parents,
    )
    value_act = causal_conv(value_prev, gate_value[:, :, 1], value_kernel, value_offset).reshape(
        steps_count, local_particles, local_heads, head_width
    )
    mixing_act = causal_conv(mixing_prev, mixing_raw, mixing_kernel, mixing_offset)
    mixing_all = lax.all_gather(mixing_act.astype(jnp.bfloat16), "head", axis=2, tiled=True).astype(
        mixing_act.dtype
    )
    per_group = head_count // GROUPS
    group_index = head_index // per_group
    input_mix = lax.dynamic_slice_in_dim(mixing_all, group_index * state_width, state_width, 2)
    output_mix = lax.dynamic_slice_in_dim(
        mixing_all, (GROUPS + group_index) * state_width, state_width, 2
    )
    step_size = jax.nn.softplus(step_raw + step_offset)
    decay = jnp.exp(-step_size * jnp.exp(decay_log))
    skip_term = skip_gain[:, None] * value_act

    def advance(state_now, inputs):
        value_now, input_now, output_now, size_now, decay_now = inputs
        state_now = (
            decay_now[:, :, None, None] * state_now
            + (size_now[:, :, None] * value_now)[..., None] * input_now[:, None, None, :]
        )
        read_out = jnp.einsum(
            "bhpn,bn->bhp", state_now, output_now, precision=lax.Precision.HIGHEST
        )
        return (state_now, read_out)

    unused_state, local_read = lax.scan(
        advance, start_state, (value_act, input_mix, output_mix, step_size, decay)
    )
    read_all = local_read + skip_term
    gated = read_all * jax.nn.silu(
        gate_value[:, :, 0].reshape(steps_count, local_particles, local_heads, head_width)
    )
    squares = jnp.sum(gated * gated, axis=(2, 3))
    selector = jnp.arange(GROUPS, dtype=jnp.int32) == group_index
    slots = jnp.where(selector, squares[..., None], 0.0)
    summed = lax.psum(slots, "head")
    group_total = jnp.sum(jnp.where(selector, summed, 0.0), axis=-1)
    square_mean = group_total / (HEADS // GROUPS * P_SIZE)
    scaled = (
        (gated * lax.rsqrt(square_mean[..., None, None] + 1e-05)).reshape(row_count, channels)
        * output_gain
    ).astype(jnp.bfloat16)
    output_terms = jnp.dot(scaled, output_weight, preferred_element_type=jnp.float32).reshape(
        steps_count, local_particles, -1
    )
    return lax.psum_scatter(
        output_terms.astype(jnp.bfloat16), "head", scatter_dimension=2, tiled=True
    )


def solution(mesh):
    return jax.shard_map(
        body,
        mesh=mesh,
        in_specs=(
            P(None, "dom", "head"),
            P(),
            P("dom", "head", None, None),
            P("dom", None, "head"),
            P("dom", None, "head"),
            P("head"),
            P(None, None, "head"),
            P(None, "head"),
            P(None, "head"),
            P(None, "head"),
            P("head"),
            P(None, "head"),
            P("head"),
            P("head"),
            P("head"),
            P("head"),
            P("head"),
            P("head", None),
        ),
        out_specs=P(None, "dom", "head"),
        check_vma=False,
    )
```

profile of v0, /device:TPU:0, one launch (start us, length us, event | category | flops | bytes accessed | tf_op | source)
XLA Modules:
  0.0 750.3 jit_solution(15983251670227247696)
XLA Ops:
  11.3 8.1 %copy.52 = bf16[1024,8,2,256]{3,1,2,0:T(8,128)(2,1)} copy(bf16[1024,8,2,256]{3,2,1,0:T(2,128)(2,1)} %bitcast.78) | data formatting | bytes 16777216
  19.4 11.5 %copy.43 = bf16[512,8192]{1,0:T(8,128)(2,1)} copy(bf16[512,8192]{0,1:T(8,128)(2,1)} %bitcast.77) | data formatting | bytes 16777216 | tf_op jit(solution)/shard_map/dot_general | solution.py:75
  30.9 25.8 %all-gather = bf16[32,1,256]{2,1,0:T(2,128)(2,1)S(1)} all-gather(bf16[1,1,256]{2,1,0:T(2,128)(2,1)S(1)} %reshape.138), channel_id=1, replica_groups=mesh['dom'=4,'head'=32] {'head'}, dimensions={0}, use_global_device_ids=true | all-gather | bytes 16896 | tf_op jit(solution)/shard_map/all_gather | solution.py:65
  56.8 12.3 %all_gather.21 = bf16[64,3,256]{2,0,1:T(8,128)(2,1)S(1)} all-gather(bf16[16,3,256]{2,0,1:T(8,128)(2,1)S(1)} %convert_element_type.52), channel_id=1, replica_groups=mesh['dom'=4,'head'=32] {'dom'}, dimensions={0}, use_global_device_ids=true | all-gather | bytes 122880 | tf_op jit(solution)/shard_map/all_gather | solution.py:99
  69.2 11.9 %all_gather.22 = bf16[64,3,64]{2,0,1:T(8,128)(2,1)S(1)} all-gather(bf16[16,3,64]{2,0,1:T(8,128)(2,1)S(1)} %convert_element_type.54), channel_id=1, replica_groups=mesh['dom'=4,'head'=32] {'dom'}, dimensions={0}, use_global_device_ids=true | all-gather | bytes 30720 | tf_op jit(solution)/shard_map/all_gather | solution.py:102
  82.7 4.3 fusion.2
  90.7 7.9 %fusion.5 = f32[24,16,2,256]{3,1,2,0:T(8,128)S(1)} fusion(bf16[2,256,8192,1]{2,1,0,3:T(8,128)(2,1)} %bitcast.79, bf16[24,16,8192]{2,1,0:T(8,128)(2,1)} %all-gather.7.cloned.1.call-done, f32[8192]{0:T(1024)S(1)} %bitcast.82, f32[24,16]{1,0:T(8,128)S(1)} %add_rsqrt_fusion.1), kind=kOutput, calls=%fused_computation.18 | convolution fusion | flops 3233808384 | bytes 15500800 | tf_op jit(solution)/shard_map/dot_general | solution.py:75
  100.4 10.4 %multiply_exponential_fusion = (f32[24,16,4]{1,2,0:T(4,128)S(1)}, f32[24,16,4]{1,2,0:T(4,128)S(1)}) fusion(f32[4]{0:T(128)S(1)} %exp.23, f32[4]{0:T(128)S(1)} %copy-done.16, bf16[8192,4]{0,1:T(4,128)(2,1)S(1)} %copy-done.13, bf16[24,16,8192]{2,1,0:T(8,128)(2,1)} %all-gather.7.cloned.1.call-done, f32[8192]{0:T(1024)S(1)} %bitcast.83, ...), kind=kOutput, calls=%fused_computation.69 | convolution fusion | flops 37762560 | bytes 6403616 | tf_op jit(solution)/shard_map/dot_general | solution.py:83
  110.8 40.1 %all-gather.5.cloned.1.call-done = bf16[64,4,64,256]{3,2,1,0:T(8,128)(2,1)} async-done(((bf16[16,4,64,256]{3,2,1,0:T(8,128)(2,1)}), bf16[64,4,64,256]{3,2,1,0:T(8,128)(2,1)}) %all-gather.5.cloned.1.call-update) | async-done | bytes 8388624 | tf_op jit(solution)/shard_map/all_gather | solution.py:96
  150.9 11.3 %convert_element_type.47 = f32[64,4,64,256]{3,2,1,0:T(8,128)} convert(bf16[64,4,64,256]{3,2,1,0:T(8,128)(2,1)} %all-gather.5.cloned.1.call-done) | non-fusion elementwise | flops 4194304 | bytes 25165824 | tf_op jit(solution)/shard_map/convert_element_type | solution.py:96
  162.2 8.9 %gather_fusion = f32[16,4,64,256]{3,2,1,0:T(8,128)} fusion(f32[64,4,64,256]{3,2,1,0:T(8,128)} %convert_element_type.47, s32[1024]{0:T(1024)S(1)} %pad_clamp_fusion), kind=kCustom, calls=%fused_computation | custom fusion | bytes 8388672 | tf_op jit(solution)/shard_map/jit(_take)/gather | solution.py:26
  171.1 5.2 select_select_fusion
  176.3 30.9 %all-gather.9.cloned.1.call-done = bf16[24,16,2048]{0,1,2:T(8,128)(2,1)} async-done(((bf16[24,16,64]{0,1,2:T(8,128)(2,1)}), bf16[24,16,2048]{0,1,2:T(8,128)(2,1)}) %all-gather.9.cloned.1.call-update) | async-done | bytes 1572880 | tf_op jit(solution)/shard_map/all_gather | solution.py:112
  207.2 4.6 convert_element_type.57
  218.0 306.0 %while.12 = (s32[]{:T(128)}, f32[16,4,64,256]{3,2,1,0:T(8,128)}, f32[24,16,4,64]{3,2,1,0:T(4,128)}, f32[24,16,4]{1,2,0:T(4,128)S(1)}, f32[24,16,4]{1,2,0:T(4,128...) while((s32[]{:T(128)}, f32[16,4,64,256]{3,2,1,0:T(8,128)}, ...), condition=%wide.region_2.3_spmd, body=%wide.region_1.2_spmd.sunk | while | flops 15732738 | bytes 12798585 | solution.py:136
  223.0 7.2 fusion.55
  231.0 4.0 multiply_add_fusion.2
  235.7 7.2 fusion.55
  248.5 7.2 fusion.55
  256.5 4.0 multiply_add_fusion.2
  261.2 7.2 fusion.55
  274.0 7.2 fusion.55
  282.0 4.0 multiply_add_fusion.2
  286.7 7.2 fusion.55
  299.5 7.2 fusion.55
  312.2 7.2 fusion.55
  325.0 7.2 fusion.55
  333.0 4.0 multiply_add_fusion.2
  337.7 7.2 fusion.55
  350.5 7.2 fusion.55
  363.2 7.2 fusion.55
  371.3 4.0 multiply_add_fusion.2
  376.0 7.2 fusion.55
  384.0 4.0 multiply_add_fusion.2
  388.7 7.2 fusion.55
  401.5 7.2 fusion.55
  414.2 7.2 fusion.55
  427.0 7.2 fusion.55
  439.7 7.2 fusion.55
  452.5 7.2 fusion.55
  465.2 7.2 fusion.55
  478.0 7.2 fusion.55
  490.7 7.2 fusion.55
  503.5 7.2 fusion.55
  516.2 7.2 fusion.55
  526.6 126.5 %psum.7 = f32[24,16,4]{1,2,0:T(4,128)S(1)} all-reduce(f32[24,16,4]{1,2,0:T(4,128)S(1)} %broadcast_select_fusion), channel_id=1, replica_groups=mesh['dom'=4,'head'=32] {'head'}, use_global_device_ids=true, to_apply=%region_4.5 | all-reduce | flops 1536 | bytes 12288 | tf_op jit(solution)/shard_map/psum | solution.py:146
  654.2 6.7 convolution_convert_fusion
  661.0 82.8 %reduce-scatter.2.cloned.1.call-done = bf16[24,16,256]{2,1,0:T(8,128)(2,1)} async-done(((bf16[24,16,8192]{2,1,0:T(8,128)(2,1)}), bf16[24,16,256]{2,1,0:T(8,128)(2,1)}) %reduce-scatter.2.cloned.1.call-update) | async-done | bytes 196624 | tf_op jit(solution)/shard_map/reduce_scatter | solution.py:156
  (265 shorter events, 131.6 us)
Async XLA Ops:
  6.5 80.5 %copy-start = (bf16[8192,64]{0,1:T(8,128)(2,1)S(1)}, bf16[8192,64]{0,1:T(8,128)(2,1)}, u32[]{:S(2)}) copy-start(bf16[8192,64]{0,1:T(8,128)(2,1)} %param.27) | copy-start | bytes 3145732
  6.5 76.1 %all-gather.7.cloned.1.call-start = ((), (), s32[]{:S(2)}) async-start(), calls=%async_computation.2 | async-start | bytes 6488064 | tf_op jit(solution)/shard_map/all_gather | solution.py:64
  7.3 143.7 %all-gather.5.cloned.1.call-start = ((), (), s32[]{:S(2)}) async-start(), calls=%async_computation.1 | async-start | bytes 10485760 | tf_op jit(solution)/shard_map/all_gather | solution.py:96
  11.2 196.0 %all-gather.9.cloned.1.call-start = ((), (), s32[]{:S(2)}) async-start(), calls=%async_computation.3 | async-start | bytes 8650752 | tf_op jit(solution)/shard_map/all_gather | solution.py:112
  19.4 11.5 %copy-start.14 = (f32[256]{0:T(256)S(1)}, f32[256]{0:T(256)}, u32[]{:S(2)}) copy-start(f32[256]{0:T(256)} %param.25) | copy-start | bytes 3076
  19.4 37.4 %copy-start.15 = (f32[4]{0:T(128)S(1)}, f32[4]{0:T(128)}, u32[]{:S(2)}) copy-start(f32[4]{0:T(128)} %param.34) | copy-start | bytes 52
  19.4 37.4 %copy-start.4 = (f32[16,3,256]{2,0,1:T(8,128)S(1)}, f32[16,3,256]{2,0,1:T(8,128)}, u32[]{:S(2)}) copy-start(f32[16,3,256]{2,0,1:T(8,128)} %param.23) | copy-start | bytes 147460
  19.4 49.8 %copy-start.5 = (f32[16,3,64]{2,0,1:T(8,128)S(1)}, f32[16,3,64]{2,0,1:T(8,128)}, u32[]{:S(2)}) copy-start(f32[16,3,64]{2,0,1:T(8,128)} %param.24) | copy-start | bytes 36868
  19.4 61.8 %copy-start.11 = (s32[64]{0:T(128)S(1)}, s32[64]{0:T(128)}, u32[]{:S(2)}) copy-start(s32[64]{0:T(128)} %param.21) | copy-start | bytes 772
  19.4 63.1 %copy-start.8 = (f32[4,64]{1,0:T(4,128)S(1)}, f32[4,64]{1,0:T(4,128)}, u32[]{:S(2)}) copy-start(f32[4,64]{1,0:T(4,128)} %param.31) | copy-start | bytes 3076
  19.4 63.1 %copy-start.6 = (f32[4,256]{1,0:T(4,128)S(1)}, f32[4,256]{1,0:T(4,128)}, u32[]{:S(2)}) copy-start(f32[4,256]{1,0:T(4,128)} %param.29) | copy-start | bytes 12292
  82.7 4.8 copy-start.2
  87.4 1.9 copy-start.10
  90.4 653.4 %reduce-scatter.2.cloned.1.call-start = ((), (), s32[]{:S(2)}) async-start(), calls=%async_computation.4 | async-start | bytes 6488064 | tf_op jit(solution)/shard_map/reduce_scatter | solution.py:156
  90.6 9.3 %copy-start.9 = (f32[256]{0:T(256)S(1)}, f32[256]{0:T(256)}, u32[]{:S(2)}) copy-start(f32[256]{0:T(256)} %param.30) | copy-start | bytes 3076
  90.6 9.8 %copy-start.13 = (bf16[8192,4]{0,1:T(4,128)(2,1)S(1)}, bf16[8192,4]{0,1:T(4,128)(2,1)}, u32[]{:S(2)}) copy-start(bf16[8192,4]{0,1:T(4,128)(2,1)} %param.28) | copy-start | bytes 196612
  90.6 9.8 %copy-start.16 = (f32[4]{0:T(128)S(1)}, f32[4]{0:T(128)}, u32[]{:S(2)}) copy-start(f32[4]{0:T(128)} %param.33) | copy-start | bytes 52
  218.0 306.0 %copy-start.3 = (f32[24,16,4,64]{3,2,1,0:T(4,128)S(1)}, f32[24,16,4,64]{3,2,1,0:T(4,128)}, u32[]{:S(2)}) copy-start(f32[24,16,4,64]{3,2,1,0:T(4,128)} %reshape_squeeze.3) | copy-start | bytes 1179652
  218.0 306.0 %copy-start.12 = (f32[4]{0:T(128)S(1)}, f32[4]{0:T(128)}, u32[]{:S(2)}) copy-start(f32[4]{0:T(128)} %param.35) | copy-start | bytes 52
  218.0 436.2 %copy-start.7 = (f32[256]{0:T(256)S(1)}, f32[256]{0:T(256)}, u32[]{:S(2)}) copy-start(f32[256]{0:T(256)} %param.36) | copy-start | bytes 3076
  654.2 89.6 %copy-start.1 = (bf16[8192,64]{0,1:T(8,128)(2,1)S(1)}, bf16[8192,64]{0,1:T(8,128)(2,1)}, u32[]{:S(2)}) copy-start(bf16[8192,64]{0,1:T(8,128)(2,1)} %param.27) | copy-start | bytes 3145732
Sparse Core Ops, SparseCore 0:
  9.5 57.0 all-gather.6
  68.3 82.6 all-gather.4
  153.2 53.9 all-gather.8
  661.1 82.6 reduce-scatter.1
where the time goes:
time: 753 us; the launch traced here: 750 us
  matrix products  199 us (26%)
  blocking collectives  177 us (24%)
  waiting for transfers between devices  155 us (21%)
  other arithmetic  131 us (17%)
  local copies, waits for them, and re-layouts  75.8 us (10%)
  between operations  13.5 us (2%)
    dot_general x24, matrix products, advance(): jnp.einsum('bhpn,bn->bhp', state_now, output_now, precision=lax.Precision...  172 us
    psum x1, blocking collectives, body(): summed = lax.psum(slots, 'head')  127 us
    add x24, other arithmetic, advance(): decay_now[:, :, None, None] * state_now  95.7 us
    reduce_scatter x1, waiting for transfers between devices, body(): lax.psum_scatter(output_terms.astype(jnp.bfloat16), 'head', scatter_dimen...  82.8 us
    all_gather x1, waiting for transfers between devices, body(): lax.all_gather(recurrent_state.astype(jnp.bfloat16), 'dom', axis=0, tiled...  40.1 us
    all_gather x1, waiting for transfers between devices, body(): lax.all_gather(mixing_act.astype(jnp.bfloat16), 'head', axis=2, tiled=True)  30.9 us
    all_gather x1, blocking collectives, body(): lax.all_gather(input_gain.astype(jnp.bfloat16), 'head', axis=0, tiled=True)  25.8 us
    squeeze x24, local copies, waits for them, and re-layouts, body(): lax.scan(advance, start_state, (value_act, input_mix, output_mix, step_si...  17.2 us
  transfers between devices with their start and end apart: 4, of which 3 were waited for; matrix products, arithmetic and copies ran while one was open for 10% of the time, Pallas kernels for 0%

commit v1 on v0

--- a/solution.py
+++ b/solution.py
@@ -6,6 +6,28 @@
 HEADS = 128
 GROUPS = 4
 P_SIZE = 64
+
+
+def laid_out(tiles, dim):
+    tiles = jnp.moveaxis(tiles, 0, dim)
+    shape = tiles.shape
+    return tiles.reshape(*shape[:dim], shape[dim] * shape[dim + 1], *shape[dim + 2 :])
+
+
+def collected_by_bits(value, axis):
+    size = lax.axis_size(axis)
+    blocks = value[None]
+    for level in range(size.bit_length() - 1):
+        stride = 1 << level
+        partner_block = lax.ppermute(blocks, axis, [(i, i ^ stride) for i in range(size)])
+        both = jnp.stack([blocks, partner_block])
+        upper = lax.axis_index(axis) >> level & 1
+        blocks = jnp.where(upper == 0, both, both[::-1]).reshape(-1, *value.shape)
+    return blocks
+
+
+def gather_by_bits(shard, axis, dim):
+    return laid_out(collected_by_bits(shard, axis), dim)
 
 
 def causal_conv(previous, current, kernel, shift_bias):
@@ -109,9 +131,7 @@
         steps_count, local_particles, local_heads, head_width
     )
     mixing_act = causal_conv(mixing_prev, mixing_raw, mixing_kernel, mixing_offset)
-    mixing_all = lax.all_gather(mixing_act.astype(jnp.bfloat16), "head", axis=2, tiled=True).astype(
-        mixing_act.dtype
-    )
+    mixing_all = gather_by_bits(mixing_act.astype(jnp.bfloat16), "head", 2).astype(mixing_act.dtype)
     per_group = head_count // GROUPS
     group_index = head_index // per_group
     input_mix = lax.dynamic_slice_in_dim(mixing_all, group_index * state_width, state_width, 2)

time: 753 us -> 696 us (0.924)
  waiting for transfers between devices: 155 us -> 114 us
  local copies, waits for them, and re-layouts: 75.8 us -> 47.1 us
  starting transfers between devices: 0.31 us -> 8.01 us
    all_gather x1, waiting for transfers between devices: 40.1 us -> 2.34 us  [body(): lax.all_gather(recurrent_state.astype(jnp.bfloat16), 'dom', axis=0, tiled...]
    all_gather x1 -> x0, waiting for transfers between devices: 30.9 us -> none  [body(): lax.all_gather(mixing_act.astype(jnp.bfloat16), 'head', axis=2, tiled=True)]
    ppermute x0 -> x5, waiting for transfers between devices: none -> 28.6 us  [collected_by_bits(): lax.ppermute(blocks, axis, [(i, i ^ stride) for i in range(size)])]
    squeeze x24, local copies, waits for them, and re-layouts: 17.2 us -> 0.05 us  [body(): lax.scan(advance, start_state, (value_act, input_mix, output_mix, step_si...]
    dynamic_update_slice x24, local copies, waits for them, and re-layouts: 14.9 us -> 0.43 us  [body(): lax.scan(advance, start_state, (value_act, input_mix, output_mix, step_si...]
    ppermute x0 -> x5, starting transfers between devices: none -> 7.92 us  [collected_by_bits(): lax.ppermute(blocks, axis, [(i, i ^ stride) for i in range(size)])]
  transfers between devices with their start and end apart: 4 -> 8, of which waited for: 3 -> 6; matrix products, arithmetic and copies ran while one was open for 10% -> 12% of each run, Pallas kernels for 0% -> 0%
where the time goes in v1:
time: 696 us; the launch traced here: 694 us
  matrix products  197 us (28%)
  blocking collectives  178 us (26%)
  other arithmetic  135 us (19%)
  waiting for transfers between devices  114 us (16%)
  local copies, waits for them, and re-layouts  47.1 us (7%)
  between operations  13.6 us (2%)
  starting transfers between devices  8.01 us (1%)
    dot_general x24, matrix products, advance(): jnp.einsum('bhpn,bn->bhp', state_now, output_now, precision=lax.Precision...  172 us
    psum x1, blocking collectives, body(): summed = lax.psum(slots, 'head')  128 us
    add x24, other arithmetic, advance(): decay_now[:, :, None, None] * state_now  96.5 us
    reduce_scatter x1, waiting for transfers between devices, body(): lax.psum_scatter(output_terms.astype(jnp.bfloat16), 'head', scatter_dimen...  82.6 us
    ppermute x5, waiting for transfers between devices, collected_by_bits(): lax.ppermute(blocks, axis, [(i, i ^ stride) for i in range(size)])  28.6 us
    all_gather x1, blocking collectives, body(): lax.all_gather(input_gain.astype(jnp.bfloat16), 'head', axis=0, tiled=True)  25.8 us
  transfers between devices with their start and end apart: 8, of which 6 were waited for; matrix products, arithmetic and copies ran while one was open for 12% of the time, Pallas kernels for 0%

profile of v1, /device:TPU:0, one launch (start us, length us, event | category | flops | bytes accessed | tf_op | source)
XLA Modules:
  0.0 694.4 jit_solution(5172714715334806974)
XLA Ops:
  11.2 8.1 %copy.54 = bf16[1024,8,2,256]{3,1,2,0:T(8,128)(2,1)} copy(bf16[1024,8,2,256]{3,2,1,0:T(2,128)(2,1)} %bitcast.106) | data formatting | bytes 16777216
  19.4 12.1 %copy.46 = bf16[512,8192]{1,0:T(8,128)(2,1)} copy(bf16[512,8192]{0,1:T(8,128)(2,1)} %bitcast.103) | data formatting | bytes 16777216 | tf_op jit(solution)/shard_map/dot_general | solution.py:97
  31.4 25.8 %all-gather = bf16[32,1,256]{2,1,0:T(2,128)(2,1)S(1)} all-gather(bf16[1,1,256]{2,1,0:T(2,128)(2,1)S(1)} %reshape.162), channel_id=1, replica_groups=mesh['dom'=4,'head'=32] {'head'}, dimensions={0}, use_global_device_ids=true | all-gather | bytes 16896 | tf_op jit(solution)/shard_map/all_gather | solution.py:87
  57.3 12.3 %all_gather.18 = bf16[64,3,256]{2,0,1:T(8,128)(2,1)S(1)} all-gather(bf16[16,3,256]{2,0,1:T(8,128)(2,1)S(1)} %convert_element_type.61), channel_id=1, replica_groups=mesh['dom'=4,'head'=32] {'dom'}, dimensions={0}, use_global_device_ids=true | all-gather | bytes 122880 | tf_op jit(solution)/shard_map/all_gather | solution.py:121
  69.7 11.9 %all_gather.19 = bf16[64,3,64]{2,0,1:T(8,128)(2,1)S(1)} all-gather(bf16[16,3,64]{2,0,1:T(8,128)(2,1)S(1)} %convert_element_type.63), channel_id=1, replica_groups=mesh['dom'=4,'head'=32] {'dom'}, dimensions={0}, use_global_device_ids=true | all-gather | bytes 30720 | tf_op jit(solution)/shard_map/all_gather | solution.py:124
  83.2 4.2 fusion.2
  87.5 4.8 fusion.8
  95.4 5.6 collective-permute-done.1
  107.0 6.1 collective-permute-done.2
  116.1 15.7 %collective-permute-done.3 = bf16[8,24,16,64]{3,2,1,0:T(8,128)(2,1)} collective-permute-done((bf16[8,24,16,64]{3,2,1,0:T(8,128)(2,1)S(1)}, bf16[8,24,16,64]{3,2,1,0:T(8,128)(2,1)}, u32[]{:S(2)}, u32[]{:S(2)}) %collective-permute-start.3) | collective-permute-done | bytes 393248 | tf_op jit(solution)/shard_map/ppermute | solution.py:22
  138.3 10.3 %multiply_exponential_fusion = (f32[24,16,4]{1,2,0:T(4,128)S(1)}, f32[24,16,4]{1,2,0:T(4,128)S(1)}) fusion(f32[4]{0:T(128)S(1)} %exp.23, f32[4]{0:T(128)S(1)} %copy-done.15, bf16[8192,4]{0,1:T(4,128)(2,1)S(1)} %copy-done.12, bf16[24,16,8192]{2,1,0:T(8,128)(2,1)} %all-gather.6.cloned.1.call-done, f32[8192]{0:T(1024)S(1)} %bitcast.122, ...), kind=kOutput, calls=%fused_computation.82 | convolution fusion | flops 37762560 | bytes 6403616 | tf_op jit(solution)/shard_map/dot_general | solution.py:105
  150.9 11.3 %convert_element_type.56 = f32[64,4,64,256]{3,2,1,0:T(8,128)} convert(bf16[64,4,64,256]{3,2,1,0:T(8,128)(2,1)} %all-gather.4.cloned.1.call-done) | non-fusion elementwise | flops 4194304 | bytes 25165824 | tf_op jit(solution)/shard_map/convert_element_type | solution.py:118
  162.2 8.5 %gather_fusion = f32[16,4,64,256]{3,2,1,0:T(8,128)} fusion(f32[64,4,64,256]{3,2,1,0:T(8,128)} %convert_element_type.56, s32[1024]{0:T(1024)S(1)} %pad_clamp_fusion), kind=kCustom, calls=%fused_computation | custom fusion | bytes 8388672 | tf_op jit(solution)/shard_map/jit(_take)/gather | solution.py:48
  170.8 5.2 select_select_fusion
  183.6 6.5 reshape.133
  191.3 276.3 %while.12 = (s32[]{:T(128)}, f32[16,4,64,256]{3,2,1,0:T(8,128)}, f32[24,16,4,64]{3,2,1,0:T(4,128)S(1)}, f32[24,16,4]{1,2,0:T(4,128)S(1)}, f32[24,16,4]{1,2,0:T(4...) while((s32[]{:T(128)}, f32[16,4,64,256]{3,2,1,0:T(8,128)}, ...), condition=%wide.region_2.3_spmd, body=%wide.region_1.2_spmd.sunk | while | flops 15732738 | bytes 12814969 | solution.py:156
  191.6 4.0 multiply_add_fusion.2
  195.6 7.2 %fusion.59 = f32[16,1,4,64]{3,1,2,0:T(1,128)S(1)} fusion(f32[16,4,64,256]{3,2,1,0:T(8,128)} %multiply_add_fusion.2, f32[16,256,1,1]{1,0,2,3:T(8,128)S(1)} %dynamic-slice_bitcast_fusion.9), kind=kOutput, calls=%fused_computation.5.clone.1 | convolution fusion | flops 12582912 | bytes 4227072 | tf_op jit(solution)/shard_map/while/body/eval_jaxpr/bhpn,bn->bhp/dot_general | solution.py:151
  203.1 4.0 multiply_add_fusion.2
  207.2 7.2 %fusion.59 = f32[16,1,4,64]{3,1,2,0:T(1,128)S(1)} fusion(f32[16,4,64,256]{3,2,1,0:T(8,128)} %multiply_add_fusion.2, f32[16,256,1,1]{1,0,2,3:T(8,128)S(1)} %dynamic-slice_bitcast_fusion.9), kind=kOutput, calls=%fused_computation.5.clone.1 | convolution fusion | flops 12582912 | bytes 4227072 | tf_op jit(solution)/shard_map/while/body/eval_jaxpr/bhpn,bn->bhp/dot_general | solution.py:151
  214.6 4.0 multiply_add_fusion.2
  218.7 7.2 %fusion.59 = f32[16,1,4,64]{3,1,2,0:T(1,128)S(1)} fusion(f32[16,4,64,256]{3,2,1,0:T(8,128)} %multiply_add_fusion.2, f32[16,256,1,1]{1,0,2,3:T(8,128)S(1)} %dynamic-slice_bitcast_fusion.9), kind=kOutput, calls=%fused_computation.5.clone.1 | convolution fusion | flops 12582912 | bytes 4227072 | tf_op jit(solution)/shard_map/while/body/eval_jaxpr/bhpn,bn->bhp/dot_general | solution.py:151
  226.2 4.0 multiply_add_fusion.2
  230.2 7.2 %fusion.59 = f32[16,1,4,64]{3,1,2,0:T(1,128)S(1)} fusion(f32[16,4,64,256]{3,2,1,0:T(8,128)} %multiply_add_fusion.2, f32[16,256,1,1]{1,0,2,3:T(8,128)S(1)} %dynamic-slice_bitcast_fusion.9), kind=kOutput, calls=%fused_computation.5.clone.1 | convolution fusion | flops 12582912 | bytes 4227072 | tf_op jit(solution)/shard_map/while/body/eval_jaxpr/bhpn,bn->bhp/dot_general | solution.py:151
  241.7 7.2 %fusion.59 = f32[16,1,4,64]{3,1,2,0:T(1,128)S(1)} fusion(f32[16,4,64,256]{3,2,1,0:T(8,128)} %multiply_add_fusion.2, f32[16,256,1,1]{1,0,2,3:T(8,128)S(1)} %dynamic-slice_bitcast_fusion.9), kind=kOutput, calls=%fused_computation.5.clone.1 | convolution fusion | flops 12582912 | bytes 4227072 | tf_op jit(solution)/shard_map/while/body/eval_jaxpr/bhpn,bn->bhp/dot_general | solution.py:151
  249.2 4.0 multiply_add_fusion.2
  253.2 7.2 %fusion.59 = f32[16,1,4,64]{3,1,2,0:T(1,128)S(1)} fusion(f32[16,4,64,256]{3,2,1,0:T(8,128)} %multiply_add_fusion.2, f32[16,256,1,1]{1,0,2,3:T(8,128)S(1)} %dynamic-slice_bitcast_fusion.9), kind=kOutput, calls=%fused_computation.5.clone.1 | convolution fusion | flops 12582912 | bytes 4227072 | tf_op jit(solution)/shard_map/while/body/eval_jaxpr/bhpn,bn->bhp/dot_general | solution.py:151
  264.7 7.2 %fusion.59 = f32[16,1,4,64]{3,1,2,0:T(1,128)S(1)} fusion(f32[16,4,64,256]{3,2,1,0:T(8,128)} %multiply_add_fusion.2, f32[16,256,1,1]{1,0,2,3:T(8,128)S(1)} %dynamic-slice_bitcast_fusion.9), kind=kOutput, calls=%fused_computation.5.clone.1 | convolution fusion | flops 12582912 | bytes 4227072 | tf_op jit(solution)/shard_map/while/body/eval_jaxpr/bhpn,bn->bhp/dot_general | solution.py:151
  276.2 7.2 %fusion.59 = f32[16,1,4,64]{3,1,2,0:T(1,128)S(1)} fusion(f32[16,4,64,256]{3,2,1,0:T(8,128)} %multiply_add_fusion.2, f32[16,256,1,1]{1,0,2,3:T(8,128)S(1)} %dynamic-slice_bitcast_fusion.9), kind=kOutput, calls=%fused_computation.5.clone.1 | convolution fusion | flops 12582912 | bytes 4227072 | tf_op jit(solution)/shard_map/while/body/eval_jaxpr/bhpn,bn->bhp/dot_general | solution.py:151
  287.7 7.2 %fusion.59 = f32[16,1,4,64]{3,1,2,0:T(1,128)S(1)} fusion(f32[16,4,64,256]{3,2,1,0:T(8,128)} %multiply_add_fusion.2, f32[16,256,1,1]{1,0,2,3:T(8,128)S(1)} %dynamic-slice_bitcast_fusion.9), kind=kOutput, calls=%fused_computation.5.clone.1 | convolution fusion | flops 12582912 | bytes 4227072 | tf_op jit(solution)/shard_map/while/body/eval_jaxpr/bhpn,bn->bhp/dot_general | solution.py:151
  299.2 7.2 %fusion.59 = f32[16,1,4,64]{3,1,2,0:T(1,128)S(1)} fusion(f32[16,4,64,256]{3,2,1,0:T(8,128)} %multiply_add_fusion.2, f32[16,256,1,1]{1,0,2,3:T(8,128)S(1)} %dynamic-slice_bitcast_fusion.9), kind=kOutput, calls=%fused_computation.5.clone.1 | convolution fusion | flops 12582912 | bytes 4227072 | tf_op jit(solution)/shard_map/while/body/eval_jaxpr/bhpn,bn->bhp/dot_general | solution.py:151
  310.8 7.2 %fusion.59 = f32[16,1,4,64]{3,1,2,0:T(1,128)S(1)} fusion(f32[16,4,64,256]{3,2,1,0:T(8,128)} %multiply_add_fusion.2, f32[16,256,1,1]{1,0,2,3:T(8,128)S(1)} %dynamic-slice_bitcast_fusion.9), kind=kOutput, calls=%fused_computation.5.clone.1 | convolution fusion | flops 12582912 | bytes 4227072 | tf_op jit(solution)/shard_map/while/body/eval_jaxpr/bhpn,bn->bhp/dot_general | solution.py:151
  322.3 7.2 %fusion.59 = f32[16,1,4,64]{3,1,2,0:T(1,128)S(1)} fusion(f32[16,4,64,256]{3,2,1,0:T(8,128)} %multiply_add_fusion.2, f32[16,256,1,1]{1,0,2,3:T(8,128)S(1)} %dynamic-slice_bitcast_fusion.9), kind=kOutput, calls=%fused_computation.5.clone.1 | convolution fusion | flops 12582912 | bytes 4227072 | tf_op jit(solution)/shard_map/while/body/eval_jaxpr/bhpn,bn->bhp/dot_general | solution.py:151
  333.8 7.2 %fusion.59 = f32[16,1,4,64]{3,1,2,0:T(1,128)S(1)} fusion(f32[16,4,64,256]{3,2,1,0:T(8,128)} %multiply_add_fusion.2, f32[16,256,1,1]{1,0,2,3:T(8,128)S(1)} %dynamic-slice_bitcast_fusion.9), kind=kOutput, calls=%fused_computation.5.clone.1 | convolution fusion | flops 12582912 | bytes 4227072 | tf_op jit(solution)/shard_map/while/body/eval_jaxpr/bhpn,bn->bhp/dot_general | solution.py:151
  345.3 7.2 %fusion.59 = f32[16,1,4,64]{3,1,2,0:T(1,128)S(1)} fusion(f32[16,4,64,256]{3,2,1,0:T(8,128)} %multiply_add_fusion.2, f32[16,256,1,1]{1,0,2,3:T(8,128)S(1)} %dynamic-slice_bitcast_fusion.9), kind=kOutput, calls=%fused_computation.5.clone.1 | convolution fusion | flops 12582912 | bytes 4227072 | tf_op jit(solution)/shard_map/while/body/eval_jaxpr/bhpn,bn->bhp/dot_general | solution.py:151
  356.8 7.2 %fusion.59 = f32[16,1,4,64]{3,1,2,0:T(1,128)S(1)} fusion(f32[16,4,64,256]{3,2,1,0:T(8,128)} %multiply_add_fusion.2, f32[16,256,1,1]{1,0,2,3:T(8,128)S(1)} %dynamic-slice_bitcast_fusion.9), kind=kOutput, calls=%fused_computation.5.clone.1 | convolution fusion | flops 12582912 | bytes 4227072 | tf_op jit(solution)/shard_map/while/body/eval_jaxpr/bhpn,bn->bhp/dot_general | solution.py:151
  368.3 7.2 %fusion.59 = f32[16,1,4,64]{3,1,2,0:T(1,128)S(1)} fusion(f32[16,4,64,256]{3,2,1,0:T(8,128)} %multiply_add_fusion.2, f32[16,256,1,1]{1,0,2,3:T(8,128)S(1)} %dynamic-slice_bitcast_fusion.9), kind=kOutput, calls=%fused_computation.5.clone.1 | convolution fusion | flops 12582912 | bytes 4227072 | tf_op jit(solution)/shard_map/while/body/eval_jaxpr/bhpn,bn->bhp/dot_general | solution.py:151
  379.8 7.2 %fusion.59 = f32[16,1,4,64]{3,1,2,0:T(1,128)S(1)} fusion(f32[16,4,64,256]{3,2,1,0:T(8,128)} %multiply_add_fusion.2, f32[16,256,1,1]{1,0,2,3:T(8,128)S(1)} %dynamic-slice_bitcast_fusion.9), kind=kOutput, calls=%fused_computation.5.clone.1 | convolution fusion | flops 12582912 | bytes 4227072 | tf_op jit(solution)/shard_map/while/body/eval_jaxpr/bhpn,bn->bhp/dot_general | solution.py:151
  391.3 7.2 %fusion.59 = f32[16,1,4,64]{3,1,2,0:T(1,128)S(1)} fusion(f32[16,4,64,256]{3,2,1,0:T(8,128)} %multiply_add_fusion.2, f32[16,256,1,1]{1,0,2,3:T(8,128)S(1)} %dynamic-slice_bitcast_fusion.9), kind=kOutput, calls=%fused_computation.5.clone.1 | convolution fusion | flops 12582912 | bytes 4227072 | tf_op jit(solution)/shard_map/while/body/eval_jaxpr/bhpn,bn->bhp/dot_general | solution.py:151
  402.9 7.2 %fusion.59 = f32[16,1,4,64]{3,1,2,0:T(1,128)S(1)} fusion(f32[16,4,64,256]{3,2,1,0:T(8,128)} %multiply_add_fusion.2, f32[16,256,1,1]{1,0,2,3:T(8,128)S(1)} %dynamic-slice_bitcast_fusion.9), kind=kOutput, calls=%fused_computation.5.clone.1 | convolution fusion | flops 12582912 | bytes 4227072 | tf_op jit(solution)/shard_map/while/body/eval_jaxpr/bhpn,bn->bhp/dot_general | solution.py:151
  414.4 7.2 %fusion.59 = f32[16,1,4,64]{3,1,2,0:T(1,128)S(1)} fusion(f32[16,4,64,256]{3,2,1,0:T(8,128)} %multiply_add_fusion.2, f32[16,256,1,1]{1,0,2,3:T(8,128)S(1)} %dynamic-slice_bitcast_fusion.9), kind=kOutput, calls=%fused_computation.5.clone.1 | convolution fusion | flops 12582912 | bytes 4227072 | tf_op jit(solution)/shard_map/while/body/eval_jaxpr/bhpn,bn->bhp/dot_general | solution.py:151
  425.9 7.2 %fusion.59 = f32[16,1,4,64]{3,1,2,0:T(1,128)S(1)} fusion(f32[16,4,64,256]{3,2,1,0:T(8,128)} %multiply_add_fusion.2, f32[16,256,1,1]{1,0,2,3:T(8,128)S(1)} %dynamic-slice_bitcast_fusion.9), kind=kOutput, calls=%fused_computation.5.clone.1 | convolution fusion | flops 12582912 | bytes 4227072 | tf_op jit(solution)/shard_map/while/body/eval_jaxpr/bhpn,bn->bhp/dot_general | solution.py:151
  437.4 7.2 %fusion.59 = f32[16,1,4,64]{3,1,2,0:T(1,128)S(1)} fusion(f32[16,4,64,256]{3,2,1,0:T(8,128)} %multiply_add_fusion.2, f32[16,256,1,1]{1,0,2,3:T(8,128)S(1)} %dynamic-slice_bitcast_fusion.9), kind=kOutput, calls=%fused_computation.5.clone.1 | convolution fusion | flops 12582912 | bytes 4227072 | tf_op jit(solution)/shard_map/while/body/eval_jaxpr/bhpn,bn->bhp/dot_general | solution.py:151
  448.9 7.2 %fusion.59 = f32[16,1,4,64]{3,1,2,0:T(1,128)S(1)} fusion(f32[16,4,64,256]{3,2,1,0:T(8,128)} %multiply_add_fusion.2, f32[16,256,1,1]{1,0,2,3:T(8,128)S(1)} %dynamic-slice_bitcast_fusion.9), kind=kOutput, calls=%fused_computation.5.clone.1 | convolution fusion | flops 12582912 | bytes 4227072 | tf_op jit(solution)/shard_map/while/body/eval_jaxpr/bhpn,bn->bhp/dot_general | solution.py:151
  460.4 7.2 %fusion.59 = f32[16,1,4,64]{3,1,2,0:T(1,128)S(1)} fusion(f32[16,4,64,256]{3,2,1,0:T(8,128)} %multiply_add_fusion.2, f32[16,256,1,1]{1,0,2,3:T(8,128)S(1)} %dynamic-slice_bitcast_fusion.9), kind=kOutput, calls=%fused_computation.5.clone.1 | convolution fusion | flops 12582912 | bytes 4227072 | tf_op jit(solution)/shard_map/while/body/eval_jaxpr/bhpn,bn->bhp/dot_general | solution.py:151
  469.1 128.4 %psum.7 = f32[24,16,4]{1,2,0:T(4,128)S(1)} all-reduce(f32[24,16,4]{1,2,0:T(4,128)S(1)} %broadcast_select_fusion), channel_id=1, replica_groups=mesh['dom'=4,'head'=32] {'head'}, use_global_device_ids=true, to_apply=%region_4.5 | all-reduce | flops 1536 | bytes 12288 | tf_op jit(solution)/shard_map/psum | solution.py:166
  598.5 6.7 convolution_convert_fusion
  605.3 82.6 %reduce-scatter.2.cloned.1.call-done = bf16[24,16,256]{2,1,0:T(8,128)(2,1)} async-done(((bf16[24,16,8192]{2,1,0:T(8,128)(2,1)}), bf16[24,16,256]{2,1,0:T(8,128)(2,1)}) %reduce-scatter.2.cloned.1.call-update) | async-done | bytes 196624 | tf_op jit(solution)/shard_map/reduce_scatter | solution.py:176
  (291 shorter events, 121.8 us)
Async XLA Ops:
  6.5 80.9 %copy-start = (bf16[8192,64]{0,1:T(8,128)(2,1)S(1)}, bf16[8192,64]{0,1:T(8,128)(2,1)}, u32[]{:S(2)}) copy-start(bf16[8192,64]{0,1:T(8,128)(2,1)} %param.27) | copy-start | bytes 3145732
  6.5 76.6 %all-gather.6.cloned.1.call-start = ((), (), s32[]{:S(2)}) async-start(), calls=%async_computation.2 | async-start | bytes 6488064 | tf_op jit(solution)/shard_map/all_gather | solution.py:86
  7.3 143.7 %all-gather.4.cloned.1.call-start = ((), (), s32[]{:S(2)}) async-start(), calls=%async_computation.1 | async-start | bytes 10485760 | tf_op jit(solution)/shard_map/all_gather | solution.py:118
  11.2 676.7 %reduce-scatter.2.cloned.1.call-start = ((), (), s32[]{:S(2)}) async-start(), calls=%async_computation.3 | async-start | bytes 6488064 | tf_op jit(solution)/shard_map/reduce_scatter | solution.py:176
  19.3 12.1 %copy-start.13 = (f32[256]{0:T(256)S(1)}, f32[256]{0:T(256)}, u32[]{:S(2)}) copy-start(f32[256]{0:T(256)} %param.25) | copy-start | bytes 3076
  19.3 37.9 %copy-start.14 = (f32[4]{0:T(128)S(1)}, f32[4]{0:T(128)}, u32[]{:S(2)}) copy-start(f32[4]{0:T(128)} %param.34) | copy-start | bytes 52
  19.3 38.0 %copy-start.3 = (f32[16,3,256]{2,0,1:T(8,128)S(1)}, f32[16,3,256]{2,0,1:T(8,128)}, u32[]{:S(2)}) copy-start(f32[16,3,256]{2,0,1:T(8,128)} %param.23) | copy-start | bytes 147460
  19.3 50.4 %copy-start.4 = (f32[16,3,64]{2,0,1:T(8,128)S(1)}, f32[16,3,64]{2,0,1:T(8,128)}, u32[]{:S(2)}) copy-start(f32[16,3,64]{2,0,1:T(8,128)} %param.24) | copy-start | bytes 36868
  19.3 62.3 %copy-start.10 = (s32[64]{0:T(128)S(1)}, s32[64]{0:T(128)}, u32[]{:S(2)}) copy-start(s32[64]{0:T(128)} %param.21) | copy-start | bytes 772
  19.3 63.6 %copy-start.8 = (f32[4,64]{1,0:T(4,128)S(1)}, f32[4,64]{1,0:T(4,128)}, u32[]{:S(2)}) copy-start(f32[4,64]{1,0:T(4,128)} %param.31) | copy-start | bytes 3076
  19.4 63.6 %copy-start.5 = (f32[4,256]{1,0:T(4,128)S(1)}, f32[4,256]{1,0:T(4,128)}, u32[]{:S(2)}) copy-start(f32[4,256]{1,0:T(4,128)} %param.29) | copy-start | bytes 12292
  83.2 20.4 %slice-start = ((s8[8388608]{0:T(1024)(128)(4,1)}), s8[4194304]{0:T(1024)(128)(4,1)S(1)}, s32[]{:S(2)}) async-start(s8[8388608]{0:T(1024)(128)(4,1)} %bitcast.107), calls=%async_computation.4 | async-start | bytes 8388608
  83.2 20.3 %slice-start.2 = ((s8[6291456]{0:T(1024)(128)(4,1)}), s8[4194304]{0:T(1024)(128)(4,1)S(1)}, s32[]{:S(2)}) async-start(s8[6291456]{0:T(1024)(128)(4,1)} %bitcast.110), calls=%async_computation.6 | async-start | bytes 8388608
  87.5 4.8 copy-start.7
  87.5 16.1 %slice-start.1 = ((s8[8388608]{0:T(1024)(128)(4,1)}), s8[4194304]{0:T(1024)(128)(4,1)S(1)}, s32[]{:S(2)}) async-start(s8[8388608]{0:T(1024)(128)(4,1)} %bitcast.107), calls=%async_computation.5 | async-start | bytes 8388608
  87.5 16.0 %slice-start.3 = ((s8[6291456]{0:T(1024)(128)(4,1)}), s8[2097152]{0:T(1024)(128)(4,1)S(1)}, s32[]{:S(2)}) async-start(s8[6291456]{0:T(1024)(128)(4,1)} %bitcast.110), calls=%async_computation.7 | async-start | bytes 4194304
  92.4 1.4 collective-permute-start
  93.9 7.0 %collective-permute-start.1 = (bf16[2,24,16,64]{3,2,1,0:T(8,128)(2,1)S(1)}, bf16[2,24,16,64]{3,2,1,0:T(8,128)(2,1)S(1)}, u32[]{:S(2)}, u32[]{:S(2)}) collective-permute-start(bf16[2,24,16,64]{3,2,1,0:T(8,128)(2,1)S(1)} %get-tuple-element.75), channel_id=1, source_target_pairs={{0,2},{1,3},{2,0},{3,1},{4,6},{5,7},{6,4},{7,5},{8,10},{9,11},{10,... | collective-permute-start | bytes 294920 | tf_op jit(solution)/shard_map/ppermute | solution.py:22
  101.1 12.0 %collective-permute-start.2 = (bf16[4,24,16,64]{3,2,1,0:T(8,128)(2,1)S(1)}, bf16[4,24,16,64]{3,2,1,0:T(8,128)(2,1)S(1)}, u32[]{:S(2)}, u32[]{:S(2)}) collective-permute-start(bf16[4,24,16,64]{3,2,1,0:T(8,128)(2,1)S(1)} %bitcast.115), channel_id=1, source_target_pairs={{0,4},{1,5},{2,6},{3,7},{4,0},{5,1},{6,2},{7,3},{8,12},{9,13},{10,... | collective-permute-start | bytes 589832 | tf_op jit(solution)/shard_map/ppermute | solution.py:22
  107.0 8.5 %copy-start.9 = (f32[256]{0:T(256)S(1)}, f32[256]{0:T(256)}, u32[]{:S(2)}) copy-start(f32[256]{0:T(256)} %param.30) | copy-start | bytes 3076
  113.5 18.3 %collective-permute-start.3 = (bf16[8,24,16,64]{3,2,1,0:T(8,128)(2,1)S(1)}, bf16[8,24,16,64]{3,2,1,0:T(8,128)(2,1)}, u32[]{:S(2)}, u32[]{:S(2)}) collective-permute-start(bf16[8,24,16,64]{3,2,1,0:T(8,128)(2,1)S(1)} %bitcast.113), channel_id=1, source_target_pairs={{0,8},{1,9},{2,10},{3,11},{4,12},{5,13},{6,14},{7,15},{8,0},{9,1},... | collective-permute-start | bytes 1179656 | tf_op jit(solution)/shard_map/ppermute | solution.py:22
  131.8 6.5 copy-start.12
  131.8 6.5 copy-start.15
  135.9 41.0 %collective-permute-start.4 = (bf16[16,24,16,64]{3,0,2,1:T(8,128)(2,1)}, bf16[16,24,16,64]{3,0,2,1:T(8,128)(2,1)}, u32[]{:S(2)}, u32[]{:S(2)}) collective-permute-start(bf16[16,24,16,64]{3,0,2,1:T(8,128)(2,1)} %copy.49), channel_id=1, source_target_pairs={{0,16},{1,17},{2,18},{3,19},{4,20},{5,21},{6,22},{7,23},{8,24},{9,... | collective-permute-start | bytes 2359304 | tf_op jit(solution)/shard_map/ppermute | solution.py:22
  183.6 7.7 %copy-start.2 = (f32[24,16,4,64]{3,2,1,0:T(4,128)S(1)}, f32[24,16,4,64]{3,2,1,0:T(4,128)}, u32[]{:S(2)}) copy-start(f32[24,16,4,64]{3,2,1,0:T(4,128)} %custom-call.6) | copy-start | bytes 1179652
  191.3 276.3 %copy-start.11 = (f32[4]{0:T(128)S(1)}, f32[4]{0:T(128)}, u32[]{:S(2)}) copy-start(f32[4]{0:T(128)} %param.35) | copy-start | bytes 52
  467.6 130.9 %copy-start.6 = (f32[256]{0:T(256)S(1)}, f32[256]{0:T(256)}, u32[]{:S(2)}) copy-start(f32[256]{0:T(256)} %param.36) | copy-start | bytes 3076
  598.5 89.3 %copy-start.1 = (bf16[8192,64]{0,1:T(8,128)(2,1)S(1)}, bf16[8192,64]{0,1:T(8,128)(2,1)}, u32[]{:S(2)}) copy-start(bf16[8192,64]{0,1:T(8,128)(2,1)} %param.27) | copy-start | bytes 3145732
Sparse Core Ops, SparseCore 0:
  9.5 57.0 all-gather.5
  68.3 82.6 all-gather.3
  605.4 82.4 reduce-scatter.1
